TPU v7x, 32 devices: a whole 2x2x4 slice. The times are simulated.
32 devices in a mesh: groups: 2 (over y), block: 16 (over z, x, core).
Axes of the slice: x: 2, y: 2, z: 4, core: 2. Of those that a mesh axis runs over, the one named last changes fastest.
Arguments:
- queries: bfloat16 [49152, 1024], P(('groups', 'block')), parts along dimension 0, may hold values from -6 to 6
- keys: bfloat16 [49152, 1024], P(('groups', 'block')), parts along dimension 0, may hold values from -16 to 16
- values: bfloat16 [49152, 1024], P(('groups', 'block')), parts along dimension 0, may hold values from -12 to 12
Outputs:
- attended: bfloat16 [49152, 1024], P(('groups', 'block')), parts along dimension 0
There are 2 independent parts, one for each index of `groups`. A program takes and returns all parts, laid end to end along the dimension named above; each array names one. Nothing has to cross between parts.
All inputs are finite; a program needn't handle non-finite values.
Results may differ from a plain program's by a relative error of at most 0.0029.
Values sent between devices are 32-bit elements; how exact they have to be, the bound alone decides.
A program may use at most 128 MiB of HBM per device.

v0:
```python
import functools

import jax
import jax.numpy as jnp
from jax import lax
from jax.experimental import pallas as pl
from jax.experimental.pallas import tpu as pltpu
from jax.sharding import PartitionSpec as P

HEADS = 8
DIM = 128
TILE = 128
F32 = jnp.float32
BF16 = jnp.bfloat16


def features(x):
    x = x.astype(F32)
    return jnp.where(x > 0.0, x + 1.0, jnp.exp(x)).astype(BF16)


def nt(a, b):
    return lax.dot_general(a, b, (((1,), (1,)), ((), ())), preferred_element_type=F32)


def tn(a, b):
    return lax.dot_general(a, b, (((0,), (0,)), ((), ())), preferred_element_type=F32)


def nn(a, b):
    return jnp.dot(a, b, preferred_element_type=F32)


def kernel(
    n, q_hbm, k_hbm, v_hbm, o_hbm, qb, kb, vb, ob, fq, fk, scores, prior,
    mine, theirs, cin, cout, xin, xout, pin, pout,
    in_sem, out_sem, t_send, t_recv, z_send, z_recv, x_send, x_recv, p_send, p_recv,
):
    rows = qb.shape[1]
    tiles = rows // TILE
    half = HEADS // 2
    levels = n // 4
    me = lax.axis_index("block")
    core = lax.rem(me, 2)
    side = lax.rem(me // 2, 2)
    level = me // 4
    twin = me + 1 - 2 * core
    across = me + 2 - 4 * side

    def cols(h):
        return pl.ds(pl.multiple_of(h * DIM, DIM), DIM)

    def load(which, src, dst, h):
        return pltpu.make_async_copy(src.at[:, cols(h)], dst.at[h], in_sem.at[which, h])

    def remote(src, dst, send, recv, i, to):
        return pltpu.make_async_remote_copy(
            src_ref=src.at[i], dst_ref=dst.at[i], send_sem=send.at[i], recv_sem=recv.at[i],
            device_id={"block": to},
        )

    def to_twin(h):
        return remote(mine, theirs, t_send, t_recv, h, twin)

    def up(i):
        return remote(cout, cin, z_send, z_recv, i, me + 4)

    def over(i):
        return remote(xout, xin, x_send, x_recv, i, across)

    def prefix(i):
        return remote(pout, pin, p_send, p_recv, i, twin)

    def store(h):
        return pltpu.make_async_copy(ob.at[h], o_hbm.at[:, cols(h)], out_sem.at[h])

    for i in range(half):
        for h in (i, i + half):
            load(0, k_hbm, kb, h).start()
            load(1, v_hbm, vb, h).start()
    for h in range(HEADS):
        load(2, q_hbm, qb, h).start()

    barrier = pltpu.get_barrier_semaphore()
    pl.semaphore_signal(barrier, inc=1, device_id={"block": twin})
    pl.semaphore_signal(barrier, inc=1, device_id={"block": across})

    @pl.when(level > 0)
    def _():
        pl.semaphore_signal(barrier, inc=1, device_id={"block": me - 4})

    @pl.when(level < levels - 1)
    def _():
        pl.semaphore_signal(barrier, inc=1, device_id={"block": me + 4})

    @pl.when(level == 0)
    def _():
        cin[...] = jnp.zeros(cin.shape, F32)

    ones = jnp.ones((TILE, DIM), BF16)

    def arrive(*heads):
        for h in heads:
            load(0, k_hbm, kb, h).wait()
            load(1, v_hbm, vb, h).wait()

    def state(h):
        total = None
        for t in range(tiles):
            at = pl.ds(t * TILE, TILE)
            f = features(kb[h, at, :])
            fk[h, at, :] = f
            add = tn(f, jnp.concatenate([vb[h, at, :], ones], axis=1))
            if t:
                prior[h, t] = total
            total = total + add if t else add
        mine[h, pl.ds(0, DIM), :] = total[:, :DIM]
        mine[h, pl.ds(DIM, 8), :] = total[:, DIM:].T[:8]

    def share(i):
        to_twin(i).start()

        @pl.when(core == 0)
        def _():
            to_twin(i + half).start()

    later = lax.broadcasted_iota(jnp.int32, (TILE, TILE), 1) > lax.broadcasted_iota(
        jnp.int32, (TILE, TILE), 0
    )

    def local(h):
        for t in range(tiles):
            at = pl.ds(t * TILE, TILE)
            f = features(qb[h, at, :])
            fq[h, at, :] = f
            sc = nt(f, fk[h, at, :])
            scores[h, at, :] = jnp.where(later, 0.0, sc).astype(BF16)

    def climb(i):
        h = core * half + i
        to_twin(h).wait_recv()

        @pl.when(level > 0)
        def _():
            up(i).wait_recv()

        below = cin[i]
        both = below + (mine[h] + theirs[h])

        @pl.when(level < levels - 1)
        def _():
            cout[i] = both
            up(i).start()

        @pl.when(side == 0)
        def _():
            xout[i] = both

        @pl.when(side == 1)
        def _():
            xout[i] = below

        over(i).start()

    def cross(i):
        over(i).wait_recv()
        pout[i] = cin[i] + xin[i]
        prefix(i).start()

    def steps(u):
        i = u - 1 - 2 * level

        @pl.when((i >= 0) & (i < half))
        def _():
            climb(i)

        j = u - 3 - 2 * level

        @pl.when((j >= 0) & (j < half))
        def _():
            cross(j)

    def finish(h, before):
        norm = jnp.broadcast_to(before[DIM : DIM + 1], (DIM, DIM)).T
        start = jnp.concatenate([before[:DIM], norm], axis=1)
        for t in range(tiles):
            at = pl.ds(t * TILE, TILE)
            w = (start + prior[h, t] if t else start).astype(BF16)
            a = jnp.concatenate([scores[h, at, :], fq[h, at, :]], axis=1)
            b = jnp.concatenate([vb[h, at, :], ones], axis=1)
            r = nn(a, jnp.concatenate([b, w], axis=0))
            d = r[:, DIM:]
            x = pl.reciprocal(d, approx=True)
            x = x * (2.0 - d * x)
            ob[h, at, :] = (r[:, :DIM] * x).astype(BF16)

    def close(i):
        own = core * half + i
        other = (1 - core) * half + i
        prefix(i).wait()

        @pl.when(core == 1)
        def _():
            to_twin(other).wait_recv()
            pout[i] = pout[i] + theirs[own]
            pin[i] = pin[i] + theirs[other]

        finish(own, pout[i])
        finish(other, pin[i])
        store(own).start()
        store(other).start()

    arrive(0, half)
    state(0)
    state(half)
    near = 2 + jnp.where(level > 0, 1, 0) + jnp.where(level < levels - 1, 1, 0)
    pl.semaphore_wait(barrier, near)
    share(0)

    @pl.loop(1, half)
    def _(u):
        arrive(u, u + half)
        state(u)
        state(u + half)
        share(u)
        steps(u)

    @pl.loop(0, half)
    def _(u):
        load(2, q_hbm, qb, 2 * u).wait()
        load(2, q_hbm, qb, 2 * u + 1).wait()
        local(2 * u)
        local(2 * u + 1)
        steps(half + u)

    first = lax.max(2 * half, half + 2 * level)

    @pl.loop(2 * half, max(2 * half, half + 2 * (levels - 1)) + half)
    def _(u):
        steps(u)
        i = u - first

        @pl.when((i >= 0) & (i < half))
        def _():
            close(i)

    @pl.loop(0, half)
    def _(i):
        to_twin(i).wait_send()

        @pl.when(core == 0)
        def _():
            to_twin(i + half).wait_send()

        @pl.when(level < levels - 1)
        def _():
            up(i).wait_send()

        over(i).wait_send()

    @pl.loop(0, HEADS)
    def _(h):
        store(h).wait()


def solution(mesh):
    n = mesh.shape["block"]

    def per_device(q, k, v):
        rows = q.shape[0]
        tiles = rows // TILE
        whole = pltpu.VMEM((HEADS, rows, DIM), BF16)
        totals = pltpu.VMEM((HEADS, DIM + 8, DIM), F32)
        parts = pltpu.VMEM((HEADS // 2, DIM + 8, DIM), F32)
        line = pltpu.SemaphoreType.DMA((HEADS // 2,))
        full = pltpu.SemaphoreType.DMA((HEADS,))
        return pl.pallas_call(
            functools.partial(kernel, n),
            out_shape=jax.ShapeDtypeStruct(q.shape, BF16),
            in_specs=[pl.BlockSpec(memory_space=pl.ANY)] * 3,
            out_specs=pl.BlockSpec(memory_space=pl.ANY),
            scratch_shapes=[
                whole, whole, whole, whole, whole, whole, whole,
                pltpu.VMEM((HEADS, tiles, DIM, 2 * DIM), F32),
                totals, totals, parts, parts, parts, parts, parts, parts,
                pltpu.SemaphoreType.DMA((3, HEADS)),
                full, full, full,
                line, line, line, line, line, line,
            ],
            compiler_params=pltpu.CompilerParams(
                collective_id=0, has_side_effects=True, vmem_limit_bytes=50 * 2**20
            ),
        )(q, k, v)

    spec = P(("groups", "block"), None)
    return jax.shard_map(
        per_device, mesh=mesh, in_specs=(spec,) * 3, out_specs=spec, check_vma=False
    )
```

profile of v0, /device:TPU:25, one launch (start us, length us, event | category | flops | bytes accessed | tf_op | source)
XLA Modules:
  0.0 25.4 jit_solution(3184716306414206941)
XLA Ops:
  0.0 23.7 %shard_map.37 = bf16[1536,1024]{1,0:T(8,128)(2,1)S(1)} custom-call(bf16[1536,1024]{1,0:T(8,128)(2,1)} %q_hbm.1, bf16[1536,1024]{1,0:T(8,128)(2,1)} %k_hbm.1, bf16[1536,1024]{1,0:T(8,128)(2,1)} %v_hbm.1), custom_call_target="tpu_custom_call" | custom-call | tf_op jit(solution)/shard_map/pallas_call | solution.py:277
  23.7 1.7 %copy.5 = bf16[1536,1024]{1,0:T(8,128)(2,1)} copy(bf16[1536,1024]{1,0:T(8,128)(2,1)S(1)} %shard_map.37) | data formatting | bytes 6291456
where the time goes:
time: 25.6 us; the launch traced here: 25.4 us
  Pallas kernels  23.7 us (93%)
  local copies, waits for them, and re-layouts  1.67 us (7%)
    pallas_call x1, Pallas kernels, per_device(): pl.pallas_call(functools.partial(kernel, n), out_shape=jax.ShapeDtypeStru...  23.7 us
    unnamed x1, local copies, waits for them, and re-layouts  1.67 us

commit v1 on v0

--- a/solution.py
+++ b/solution.py
@@ -10,6 +10,9 @@
 HEADS = 8
 DIM = 128
 TILE = 128
+WIDE = 256
+CUT = DIM // 2
+CHUNKS = ((0, CUT + 8), (CUT + 8, CUT))
 F32 = jnp.float32
 BF16 = jnp.bfloat16
 
@@ -53,23 +56,24 @@
     def load(which, src, dst, h):
         return pltpu.make_async_copy(src.at[:, cols(h)], dst.at[h], in_sem.at[which, h])
 
-    def remote(src, dst, send, recv, i, to):
+    def remote(src, dst, send, recv, i, p, to):
+        at = pl.ds(*CHUNKS[p])
         return pltpu.make_async_remote_copy(
-            src_ref=src.at[i], dst_ref=dst.at[i], send_sem=send.at[i], recv_sem=recv.at[i],
-            device_id={"block": to},
+            src_ref=src.at[i, at], dst_ref=dst.at[i, at], send_sem=send.at[i, p],
+            recv_sem=recv.at[i, p], device_id={"block": to},
         )
 
-    def to_twin(h):
-        return remote(mine, theirs, t_send, t_recv, h, twin)
-
-    def up(i):
-        return remote(cout, cin, z_send, z_recv, i, me + 4)
-
-    def over(i):
-        return remote(xout, xin, x_send, x_recv, i, across)
-
-    def prefix(i):
-        return remote(pout, pin, p_send, p_recv, i, twin)
+    def to_twin(h, p):
+        return remote(mine, theirs, t_send, t_recv, h, p, twin)
+
+    def up(i, p):
+        return remote(cout, cin, z_send, z_recv, i, p, me + 4)
+
+    def over(i, p):
+        return remote(xout, xin, x_send, x_recv, i, p, across)
+
+    def prefix(i, p):
+        return remote(pout, pin, p_send, p_recv, i, p, twin)
 
     def store(h):
         return pltpu.make_async_copy(ob.at[h], o_hbm.at[:, cols(h)], out_sem.at[h])
@@ -97,92 +101,102 @@
     def _():
         cin[...] = jnp.zeros(cin.shape, F32)
 
-    ones = jnp.ones((TILE, DIM), BF16)
-
     def arrive(*heads):
         for h in heads:
             load(0, k_hbm, kb, h).wait()
             load(1, v_hbm, vb, h).wait()
 
     def state(h):
+        ones = jnp.ones((WIDE, DIM), BF16)
         total = None
-        for t in range(tiles):
-            at = pl.ds(t * TILE, TILE)
+        for t in range(rows // WIDE):
+            at = pl.ds(t * WIDE, WIDE)
             f = features(kb[h, at, :])
             fk[h, at, :] = f
             add = tn(f, jnp.concatenate([vb[h, at, :], ones], axis=1))
-            if t:
-                prior[h, t] = total
             total = total + add if t else add
-        mine[h, pl.ds(0, DIM), :] = total[:, :DIM]
-        mine[h, pl.ds(DIM, 8), :] = total[:, DIM:].T[:8]
+        mine[h, pl.ds(0, CUT), :] = total[:CUT, :DIM]
+        mine[h, pl.ds(CUT, 8), :] = total[:, DIM:].T[:8]
+        mine[h, pl.ds(CUT + 8, CUT), :] = total[CUT:, :DIM]
 
     def share(i):
-        to_twin(i).start()
+        for p in range(2):
+            to_twin(i, p).start()
 
         @pl.when(core == 0)
         def _():
-            to_twin(i + half).start()
-
+            for p in range(2):
+                to_twin(i + half, p).start()
+
+    ones = jnp.ones((TILE, DIM), BF16)
     later = lax.broadcasted_iota(jnp.int32, (TILE, TILE), 1) > lax.broadcasted_iota(
         jnp.int32, (TILE, TILE), 0
     )
 
     def local(h):
+        total = None
         for t in range(tiles):
             at = pl.ds(t * TILE, TILE)
             f = features(qb[h, at, :])
             fq[h, at, :] = f
             sc = nt(f, fk[h, at, :])
             scores[h, at, :] = jnp.where(later, 0.0, sc).astype(BF16)
+            if t < tiles - 1:
+                add = tn(fk[h, at, :], jnp.concatenate([vb[h, at, :], ones], axis=1))
+                total = total + add if t else add
+                prior[h, t + 1] = total
 
     def climb(i):
         h = core * half + i
-        to_twin(h).wait_recv()
-
+        for p in range(2):
+            at = pl.ds(*CHUNKS[p])
+            to_twin(h, p).wait_recv()
+
+            @pl.when(level > 0)
+            def _():
+                up(i, p).wait_recv()
+
+            below = cin[i, at]
+            both = below + (mine[h, at] + theirs[h, at])
+
+            @pl.when(level < levels - 1)
+            def _():
+                cout[i, at] = both
+                up(i, p).start()
+
+            @pl.when(side == 0)
+            def _():
+                xout[i, at] = both
+
+            @pl.when(side == 1)
+            def _():
+                xout[i, at] = below
+
+            over(i, p).start()
+
+    def cross(i):
+        for p in range(2):
+            at = pl.ds(*CHUNKS[p])
+            over(i, p).wait_recv()
+            pout[i, at] = cin[i, at] + xin[i, at]
+            prefix(i, p).start()
+
+    def at_turn(t, step):
+        @pl.when((t >= 0) & (t < 2 * half) & (lax.rem(t, 2) == 0))
+        def _():
+            step(lax.div(t, 2))
+
+    def steps(u):
         @pl.when(level > 0)
         def _():
-            up(i).wait_recv()
-
-        below = cin[i]
-        both = below + (mine[h] + theirs[h])
-
-        @pl.when(level < levels - 1)
-        def _():
-            cout[i] = both
-            up(i).start()
-
-        @pl.when(side == 0)
-        def _():
-            xout[i] = both
-
-        @pl.when(side == 1)
-        def _():
-            xout[i] = below
-
-        over(i).start()
-
-    def cross(i):
-        over(i).wait_recv()
-        pout[i] = cin[i] + xin[i]
-        prefix(i).start()
-
-    def steps(u):
-        i = u - 1 - 2 * level
-
-        @pl.when((i >= 0) & (i < half))
-        def _():
-            climb(i)
-
-        j = u - 3 - 2 * level
-
-        @pl.when((j >= 0) & (j < half))
-        def _():
-            cross(j)
+            at_turn(u - 3 - 2 * level, climb)
+
+        at_turn(u - 5 - 2 * level, cross)
 
     def finish(h, before):
-        norm = jnp.broadcast_to(before[DIM : DIM + 1], (DIM, DIM)).T
-        start = jnp.concatenate([before[:DIM], norm], axis=1)
+        norm = jnp.broadcast_to(before[CUT : CUT + 1], (DIM, DIM)).T
+        state = jnp.concatenate([before[:CUT], before[CUT + 8 :]], axis=0)
+        start = jnp.concatenate([state, norm], axis=1)
         for t in range(tiles):
             at = pl.ds(t * TILE, TILE)
             w = (start + prior[h, t] if t else start).astype(BF16)
@@ -197,11 +211,13 @@
     def close(i):
         own = core * half + i
         other = (1 - core) * half + i
-        prefix(i).wait()
+        for p in range(2):
+            prefix(i, p).wait()
 
         @pl.when(core == 1)
         def _():
-            to_twin(other).wait_recv()
+            for p in range(2):
+                to_twin(other, p).wait_recv()
             pout[i] = pout[i] + theirs[own]
             pin[i] = pin[i] + theirs[other]
 
@@ -223,40 +239,44 @@
         state(u)
         state(u + half)
         share(u)
+
+        @pl.when(level == 0)
+        def _():
+            climb(u - 1)
+
+    @pl.when(level == 0)
+    def _():
+        climb(half - 1)
+
+    tail = half + HEADS
+
+    @pl.loop(half, tail)
+    def _(u):
+        load(2, q_hbm, qb, u - half).wait()
+        local(u - half)
         steps(u)
 
-    @pl.loop(0, half)
-    def _(u):
-        load(2, q_hbm, qb, 2 * u).wait()
-        load(2, q_hbm, qb, 2 * u + 1).wait()
-        local(2 * u)
-        local(2 * u + 1)
-        steps(half + u)
-
-    first = lax.max(2 * half, half + 2 * level)
-
-    @pl.loop(2 * half, max(2 * half, half + 2 * (levels - 1)) + half)
+    first = lax.max(tail, 7 + 2 * level)
+
+    @pl.loop(tail, max(tail, 5 + 2 * levels) + 2 * half)
     def _(u):
         steps(u)
-        i = u - first
-
-        @pl.when((i >= 0) & (i < half))
-        def _():
-            close(i)
+        at_turn(u - first, close)
 
     @pl.loop(0, half)
     def _(i):
-        to_twin(i).wait_send()
-
-        @pl.when(core == 0)
-        def _():
-            to_twin(i + half).wait_send()
-
-        @pl.when(level < levels - 1)
-        def _():
-            up(i).wait_send()
-
-        over(i).wait_send()
+        for p in range(2):
+            to_twin(i, p).wait_send()
+
+            @pl.when(core == 0)
+            def _():
+                to_twin(i + half, p).wait_send()
+
+            @pl.when(level < levels - 1)
+            def _():
+                up(i, p).wait_send()
+
+            over(i, p).wait_send()
 
     @pl.loop(0, HEADS)
     def _(h):
@@ -272,8 +292,8 @@
         whole = pltpu.VMEM((HEADS, rows, DIM), BF16)
         totals = pltpu.VMEM((HEADS, DIM + 8, DIM), F32)
         parts = pltpu.VMEM((HEADS // 2, DIM + 8, DIM), F32)
-        line = pltpu.SemaphoreType.DMA((HEADS // 2,))
-        full = pltpu.SemaphoreType.DMA((HEADS,))
+        line = pltpu.SemaphoreType.DMA((HEADS // 2, 2))
+        full = pltpu.SemaphoreType.DMA((HEADS, 2))
         return pl.pallas_call(
             functools.partial(kernel, n),
             out_shape=jax.ShapeDtypeStruct(q.shape, BF16),
@@ -284,7 +304,8 @@
                 pltpu.VMEM((HEADS, tiles, DIM, 2 * DIM), F32),
                 totals, totals, parts, parts, parts, parts, parts, parts,
                 pltpu.SemaphoreType.DMA((3, HEADS)),
-                full, full, full,
+                pltpu.SemaphoreType.DMA((HEADS,)),
+                full, full,
                 line, line, line, line, line, line,
             ],
             compiler_params=pltpu.CompilerParams(

time: 25.6 us -> 26 us (1.016)
  the two profiles are of different devices: /device:TPU:25 before, /device:TPU:27 now
where the time goes in v1:
time: 26 us; the launch traced here: 25.9 us
  Pallas kernels  24.2 us (93%)
  local copies, waits for them, and re-layouts  1.67 us (6%)
    pallas_call x1, Pallas kernels, per_device(): pl.pallas_call(functools.partial(kernel, n), out_shape=jax.ShapeDtypeStru...  24.2 us
    unnamed x1, local copies, waits for them, and re-layouts  1.67 us

profile of v1, /device:TPU:27, one launch (start us, length us, event | category | flops | bytes accessed | tf_op | source)
XLA Modules:
  0.0 25.9 jit_solution(7089664919415346159)
XLA Ops:
  0.0 24.2 %shard_map.37 = bf16[1536,1024]{1,0:T(8,128)(2,1)S(1)} custom-call(bf16[1536,1024]{1,0:T(8,128)(2,1)} %q_hbm.1, bf16[1536,1024]{1,0:T(8,128)(2,1)} %k_hbm.1, bf16[1536,1024]{1,0:T(8,128)(2,1)} %v_hbm.1), custom_call_target="tpu_custom_call" | custom-call | tf_op jit(solution)/shard_map/pallas_call | solution.py:297
  24.2 1.7 %copy.5 = bf16[1536,1024]{1,0:T(8,128)(2,1)} copy(bf16[1536,1024]{1,0:T(8,128)(2,1)S(1)} %shard_map.37) | data formatting | bytes 6291456
